TPU v7x, 512 devices: a whole 4x8x8 slice. The times are simulated.
512 devices in a mesh: seq: 128 (over z, y, x_hi), rep: 4 (over x_lo, core).
Axes of the slice: x: 4 (x_hi: 2, x_lo: 2; x = x_hi * 2 + x_lo), y: 8, z: 8, core: 2. Of those that a mesh axis runs over, the one named last changes fastest.
Arguments:
- queries: bfloat16 [4, 128, 512, 512], P('rep', 'seq'), may hold values from -128 to 128, as said below
- key_vectors: bfloat16 [4, 128, 512, 512], P('rep', 'seq'), may hold values from -6 to 6
- value_vectors: bfloat16 [4, 128, 512, 512], P('rep', 'seq'), may hold values from -6 to 6
- out_grad: bfloat16 [4, 128, 512, 1024], P('rep', 'seq'), may hold values from -6 to 6
- out_weight: bfloat16 [512, 1024], P('seq'), may hold values from -0.25 to 0.25
- row_blocks: int32 [8, 8], replicated, may hold values from 0 to 1, as said below
- column_blocks: int32 [8, 8], replicated, may hold values from 0 to 1, as said below
Outputs:
- query_grad: bfloat16 [4, 128, 512, 512], P('rep', 'seq')
- key_grad: bfloat16 [4, 128, 512, 512], P('rep', 'seq')
- value_grad: bfloat16 [4, 128, 512, 512], P('rep', 'seq')
- weight_grad: float32 [512, 1024], P('seq')
Inputs may be any that keep to these rules, and one draw needn't show every extreme that they name: `queries`: query draws may carry large values at some positions. `row_blocks`: entry (i, j) is 1 on the diagonal, 0 above it, 0 or 1 below it. `column_blocks`: entry (i, j) is 1 on the diagonal, 0 above it, 0 or 1 below it.
All inputs are finite; a program needn't handle non-finite values.
Results may differ from a plain program's by a relative error of at most 0.0058.
Values may be sent and summed in bfloat16 or wider, within the bound.
A program may use at most 64 MiB of HBM per device.

v0:
```python
import math

import jax
import jax.numpy as jnp
from jax import lax
from jax.sharding import PartitionSpec as P

HEAD_DIM = 128
HEADS_ROW = 2
HEADS_STR = 2


def allowed_table(blocks, length):
    number_blocks = blocks.shape[0]
    block_width = length // number_blocks
    places = jnp.arange(length) // block_width
    onehot = (places[:, None] == jnp.arange(number_blocks)[None, :]).astype(jnp.float32)
    spread = jnp.dot(jnp.dot(onehot, blocks.astype(jnp.float32)), onehot.T)
    causal = jnp.arange(length)[None, :] <= jnp.arange(length)[:, None]
    return (spread > 0.5) & causal


def forward_pass(query_in, key_in, value_in, allowed, layout):
    key_layout = layout.replace("q", "k")
    scores = jnp.einsum(
        layout + "," + key_layout + "->nhqk", query_in, key_in, preferred_element_type=jnp.float32
    ) * (1.0 / math.sqrt(HEAD_DIM))
    masked = jnp.where(allowed, scores, -1e30)
    topmost = jnp.max(masked, axis=-1, keepdims=True)
    raised = jnp.exp(masked - topmost)
    attn_probs = raised / jnp.sum(raised, axis=-1, keepdims=True)
    prob_round = attn_probs.astype(jnp.bfloat16)
    outputs = jnp.einsum(
        "nhqk," + key_layout + "->" + layout,
        prob_round,
        value_in,
        preferred_element_type=jnp.float32,
    ).astype(jnp.bfloat16)
    return (attn_probs, prob_round, outputs)


def backward_pass(attn_probs, prob_round, query_in, key_in, value_in, out_cot, layout):
    key_layout = layout.replace("q", "k")
    prob_grad = jnp.einsum(
        layout + "," + key_layout + "->nhqk", out_cot, value_in, preferred_element_type=jnp.float32
    )
    inner_sum = jnp.sum(attn_probs * prob_grad, axis=-1, keepdims=True)
    score_grad = (attn_probs * (prob_grad - inner_sum) * (1.0 / math.sqrt(HEAD_DIM))).astype(
        jnp.bfloat16
    )
    value_grad = jnp.einsum(
        "nhqk," + layout + "->" + key_layout,
        prob_round,
        out_cot,
        preferred_element_type=jnp.float32,
    ).astype(jnp.bfloat16)
    query_grad = jnp.einsum(
        "nhqk," + key_layout + "->" + layout, score_grad, key_in, preferred_element_type=jnp.float32
    ).astype(jnp.bfloat16)
    key_grad = jnp.einsum(
        "nhqk," + layout + "->" + key_layout,
        score_grad,
        query_in,
        preferred_element_type=jnp.float32,
    ).astype(jnp.bfloat16)
    return (query_grad, key_grad, value_grad)


def body(queries, key_vectors, value_vectors, out_grad, out_weight, row_blocks, column_blocks):
    seq_count = lax.axis_size("seq")
    local_rows = queries.shape[1]
    columns = queries.shape[2]
    features = queries.shape[3]
    all_rows = local_rows * seq_count
    row_width = HEADS_ROW * HEAD_DIM
    strided_width = HEADS_STR * HEAD_DIM
    token_count = local_rows * columns
    flat_grad = out_grad.reshape(token_count, out_grad.shape[3])
    attn_grad = lax.dot_general(
        flat_grad,
        lax.all_gather(out_weight, "seq", axis=0, tiled=True),
        (((1,), (1,)), ((), ())),
        preferred_element_type=jnp.float32,
    )
    attn_grad = attn_grad.astype(jnp.bfloat16).reshape(queries.shape)

    def row_view(tensor):
        return tensor[0, :, :, :row_width].reshape(local_rows, columns, HEADS_ROW, HEAD_DIM)

    row_allowed = allowed_table(row_blocks, columns)
    row_query = row_view(queries)
    row_key = row_view(key_vectors)
    row_value = row_view(value_vectors)
    row_probs, row_round, row_out = forward_pass(row_query, row_key, row_value, row_allowed, "nqhd")
    row_grads = backward_pass(
        row_probs, row_round, row_query, row_key, row_value, row_view(attn_grad), "nqhd"
    )
    column_allowed = allowed_table(column_blocks, all_rows)

    def column_view(tensor):
        return tensor.reshape(all_rows, tensor.shape[2], HEADS_STR, HEAD_DIM)

    def column_back(tensor):
        return tensor.reshape(1, all_rows, tensor.shape[1], strided_width)

    moved_query, moved_key, moved_value = (
        lax.all_to_all(queries[..., row_width:], "seq", split_axis=2, concat_axis=1, tiled=True),
        lax.all_to_all(
            key_vectors[..., row_width:], "seq", split_axis=2, concat_axis=1, tiled=True
        ),
        lax.all_to_all(
            value_vectors[..., row_width:], "seq", split_axis=2, concat_axis=1, tiled=True
        ),
    )
    col_query = column_view(moved_query)
    col_key = column_view(moved_key)
    col_value = column_view(moved_value)
    col_probs, col_round, col_out = forward_pass(
        col_query, col_key, col_value, column_allowed, "qnhd"
    )
    moved_grad = lax.all_to_all(
        attn_grad[..., row_width:], "seq", split_axis=2, concat_axis=1, tiled=True
    )
    col_grads = backward_pass(
        col_probs, col_round, col_query, col_key, col_value, column_view(moved_grad), "qnhd"
    )
    column_results = tuple((column_back(tensor) for tensor in (col_out,) + col_grads))
    back_out, back_query, back_key, back_value = (
        lax.all_to_all(column_results[0], "seq", split_axis=1, concat_axis=2, tiled=True),
        lax.all_to_all(column_results[1], "seq", split_axis=1, concat_axis=2, tiled=True),
        lax.all_to_all(column_results[2], "seq", split_axis=1, concat_axis=2, tiled=True),
        lax.all_to_all(column_results[3], "seq", split_axis=1, concat_axis=2, tiled=True),
    )

    def merge_heads(row_part, back_part):
        return jnp.concatenate(
            (row_part.reshape(1, local_rows, columns, row_width), back_part), axis=3
        )

    attention = merge_heads(row_out, back_out)
    query_grad = merge_heads(row_grads[0], back_query)
    key_grad = merge_heads(row_grads[1], back_key)
    value_grad = merge_heads(row_grads[2], back_value)
    flat_out = attention.reshape(token_count, features)
    factor = 1.0 / math.sqrt(lax.axis_size("rep") * all_rows * columns)
    share_rows = features // seq_count
    full_term = (
        lax.dot_general(
            flat_out, flat_grad, (((0,), (0,)), ((), ())), preferred_element_type=jnp.float32
        )
        * factor
    )
    summed = lax.psum(full_term, ("seq", "rep"))
    weight_grad = lax.dynamic_slice_in_dim(
        summed, lax.axis_index("seq") * share_rows, share_rows, 0
    )
    return (query_grad, key_grad, value_grad, weight_grad)


def solution(mesh):
    return jax.shard_map(
        body,
        mesh=mesh,
        in_specs=(
            P("rep", "seq", None, None),
            P("rep", "seq", None, None),
            P("rep", "seq", None, None),
            P("rep", "seq", None, None),
            P("seq", None),
            P(),
            P(),
        ),
        out_specs=(
            P("rep", "seq", None, None),
            P("rep", "seq", None, None),
            P("rep", "seq", None, None),
            P("seq", None),
        ),
        check_vma=False,
    )
```

profile of v0, /device:TPU:1, one launch (start us, length us, event | category | flops | bytes accessed | tf_op | source)
XLA Modules:
  0.0 487.5 jit_solution(3546777956949517010)
XLA Ops:
  13.2 20.9 %all-to-all-start = ((bf16[128,2,512]{2,1,0:T(2,128)(2,1)}), bf16[128,2,512]{2,1,0:T(2,128)(2,1)S(1)}, u32[]{:S(2)}, u32[]{:S(2)}) async-start(bf16[128,2,512]{2,1,0:T(2,128)(2,1)} %reshape.209), calls=%async_computation | async-start | bytes 524288 | tf_op jit(solution)/shard_map/all_to_all | solution.py:107
  35.4 2.2 reduce.14
  38.5 9.8 %all-to-all-done = bf16[128,2,512]{2,1,0:T(2,128)(2,1)S(1)} async-done(((bf16[128,2,512]{2,1,0:T(2,128)(2,1)}), bf16[128,2,512]{2,1,0:T(2,128)(2,1)S(1)}, u32[]{:S(2)}, u32[]{:S(2)}) %all-to-all-start) | async-done | bytes 262176 | tf_op jit(solution)/shard_map/all_to_all | solution.py:107
  48.2 7.7 %all-to-all-start.1 = ((bf16[128,2,512]{2,1,0:T(2,128)(2,1)}), bf16[128,2,512]{2,1,0:T(2,128)(2,1)S(1)}, u32[]{:S(2)}, u32[]{:S(2)}) async-start(bf16[128,2,512]{2,1,0:T(2,128)(2,1)} %reshape.203), calls=%async_computation.1 | async-start | bytes 524288 | tf_op jit(solution)/shard_map/all_to_all | solution.py:108
  58.0 2.2 reduce.16
  61.1 8.3 %all-to-all-done.1 = bf16[128,2,512]{2,1,0:T(2,128)(2,1)S(1)} async-done(((bf16[128,2,512]{2,1,0:T(2,128)(2,1)}), bf16[128,2,512]{2,1,0:T(2,128)(2,1)S(1)}, u32[]{:S(2)}, u32[]{:S(2)}) %all-to-all-start.1) | async-done | bytes 262176 | tf_op jit(solution)/shard_map/all_to_all | solution.py:108
  69.4 8.5 %all-to-all-start.3 = ((bf16[128,2,512]{2,1,0:T(2,128)(2,1)}), bf16[128,2,512]{2,1,0:T(2,128)(2,1)S(1)}, u32[]{:S(2)}, u32[]{:S(2)}) async-start(bf16[128,2,512]{2,1,0:T(2,128)(2,1)} %reshape.207), calls=%async_computation.3 | async-start | bytes 524288 | tf_op jit(solution)/shard_map/all_to_all | solution.py:111
  84.7 6.7 %all-to-all-done.3 = bf16[128,2,512]{2,1,0:T(2,128)(2,1)S(1)} async-done(((bf16[128,2,512]{2,1,0:T(2,128)(2,1)}), bf16[128,2,512]{2,1,0:T(2,128)(2,1)S(1)}, u32[]{:S(2)}, u32[]{:S(2)}) %all-to-all-start.3) | async-done | bytes 262176 | tf_op jit(solution)/shard_map/all_to_all | solution.py:111
  95.9 9.1 %all-to-all-start.7 = ((bf16[1,128,4,256]{3,2,0,1:T(4,128)(2,1)}), bf16[1,128,4,256]{3,2,0,1:T(4,128)(2,1)S(1)}, u32[]{:S(2)}, u32[]{:S(2)}) async-start(bf16[1,128,4,256]{3,2,0,1:T(4,128)(2,1)} %copy.106), calls=%async_computation.7 | async-start | bytes 524288 | tf_op jit(solution)/shard_map/all_to_all | solution.py:129
  104.9 3.3 fusion.82
  108.4 49.2 %all-gather.3.cloned.1.call-done = bf16[128,4,1024]{2,1,0:T(4,128)(2,1)} async-done(((bf16[1,4,1024]{2,1,0:T(4,128)(2,1)}), bf16[128,4,1024]{2,1,0:T(4,128)(2,1)}) %all-gather.3.cloned.1.call-update) | async-done | bytes 1048592 | tf_op jit(solution)/shard_map/all_gather | solution.py:81
  160.8 2.2 reduce.15
  163.9 10.7 %all-to-all-start.2 = ((bf16[128,2,512]{2,1,0:T(2,128)(2,1)}), bf16[128,2,512]{2,1,0:T(2,128)(2,1)S(1)}, u32[]{:S(2)}, u32[]{:S(2)}) async-start(bf16[128,2,512]{2,1,0:T(2,128)(2,1)} %reshape.205), calls=%async_computation.2 | async-start | bytes 524288 | tf_op jit(solution)/shard_map/all_to_all | solution.py:121
  174.7 2.2 convolution_convert_fusion.2
  179.2 9.0 %all-to-all-done.2 = bf16[128,2,512]{2,1,0:T(2,128)(2,1)S(1)} async-done(((bf16[128,2,512]{2,1,0:T(2,128)(2,1)}), bf16[128,2,512]{2,1,0:T(2,128)(2,1)S(1)}, u32[]{:S(2)}, u32[]{:S(2)}) %all-to-all-start.2) | async-done | bytes 262176 | tf_op jit(solution)/shard_map/all_to_all | solution.py:121
  193.1 7.5 %all-to-all-start.5 = ((bf16[1,128,4,256]{3,2,0,1:T(4,128)(2,1)}), bf16[1,128,4,256]{3,2,0,1:T(4,128)(2,1)}, u32[]{:S(2)}, u32[]{:S(2)}) async-start(bf16[1,128,4,256]{3,2,0,1:T(4,128)(2,1)} %copy.96), calls=%async_computation.5 | async-start | bytes 524288 | tf_op jit(solution)/shard_map/all_to_all | solution.py:131
  202.0 2.7 convolution_convert_fusion.3
  206.5 7.4 %all-to-all-done.5 = bf16[1,128,4,256]{3,2,0,1:T(4,128)(2,1)} async-done(((bf16[1,128,4,256]{3,2,0,1:T(4,128)(2,1)}), bf16[1,128,4,256]{3,2,0,1:T(4,128)(2,1)}, u32[]{:S(2)}, u32[]{:S(2)}) %all-to-all-start.5) | async-done | bytes 262176 | tf_op jit(solution)/shard_map/all_to_all | solution.py:131
  213.9 8.7 %all-to-all-start.4 = ((bf16[1,128,4,256]{3,2,0,1:T(4,128)(2,1)}), bf16[1,128,4,256]{3,2,0,1:T(4,128)(2,1)}, u32[]{:S(2)}, u32[]{:S(2)}) async-start(bf16[1,128,4,256]{3,2,0,1:T(4,128)(2,1)} %copy.91), calls=%async_computation.4 | async-start | bytes 524288 | tf_op jit(solution)/shard_map/all_to_all | solution.py:130
  222.6 4.0 fusion.22
  228.4 3.9 fusion.25
  236.0 15.3 %all-to-all-start.6 = ((bf16[1,128,4,256]{3,2,0,1:T(4,128)(2,1)}), bf16[1,128,4,256]{3,2,0,1:T(4,128)(2,1)S(1)}, u32[]{:S(2)}, u32[]{:S(2)}) async-start(bf16[1,128,4,256]{3,2,0,1:T(4,128)(2,1)} %copy.101), calls=%async_computation.6 | async-start | bytes 524288 | tf_op jit(solution)/shard_map/all_to_all | solution.py:132
  251.4 2.4 convolution_convert_fusion.5
  254.0 219.9 %all-reduce.2.cloned.1.call-done = f32[512,1024]{1,0:T(8,128)} async-done(((f32[512,1024]{1,0:T(8,128)}), f32[512,1024]{1,0:T(8,128)}) %all-reduce.2.cloned.1.call-update) | async-done | bytes 2097168 | tf_op jit(solution)/shard_map/psum | solution.py:153
  (104 shorter events, 47.6 us)
Async XLA Ops:
  8.0 150.9 %copy-start = (bf16[1,1,512,1024]{3,2,1,0:T(8,128)(2,1)S(1)}, bf16[1,1,512,1024]{3,2,1,0:T(8,128)(2,1)}, u32[]{:S(2)}) copy-start(bf16[1,1,512,1024]{3,2,1,0:T(8,128)(2,1)} %param.10) | copy-start | bytes 3145732
  8.0 26.9 %copy-start.7 = (bf16[1,1,512,512]{3,2,1,0:T(8,128)(2,1)S(1)}, bf16[1,1,512,512]{3,2,1,0:T(8,128)(2,1)}, u32[]{:S(2)}) copy-start(bf16[1,1,512,512]{3,2,1,0:T(8,128)(2,1)} %param.8) | copy-start | bytes 1572868
  13.2 42.7 %copy-start.14 = (s32[8,8]{1,0:T(8,128)S(1)}, s32[8,8]{1,0:T(8,128)}, u32[]{:S(2)}) copy-start(s32[8,8]{1,0:T(8,128)} %param.13) | copy-start | bytes 772
  13.2 35.0 %all-to-all-start = ((bf16[128,2,512]{2,1,0:T(2,128)(2,1)}), bf16[128,2,512]{2,1,0:T(2,128)(2,1)S(1)}, u32[]{:S(2)}, u32[]{:S(2)}) async-start(bf16[128,2,512]{2,1,0:T(2,128)(2,1)} %reshape.209), calls=%async_computation | async-start | bytes 524288 | tf_op jit(solution)/shard_map/all_to_all | solution.py:107
  34.2 123.4 %all-gather.3.cloned.1.call-start = ((), (), s32[]{:S(2)}) async-start(), calls=%async_computation.9 | async-start | bytes 1056768 | tf_op jit(solution)/shard_map/all_gather | solution.py:81
  38.5 39.5 %copy-start.15 = (s32[8,8]{1,0:T(8,128)S(1)}, s32[8,8]{1,0:T(8,128)}, u32[]{:S(2)}) copy-start(s32[8,8]{1,0:T(8,128)} %param.12) | copy-start | bytes 772
  48.2 21.2 %all-to-all-start.1 = ((bf16[128,2,512]{2,1,0:T(2,128)(2,1)}), bf16[128,2,512]{2,1,0:T(2,128)(2,1)S(1)}, u32[]{:S(2)}, u32[]{:S(2)}) async-start(bf16[128,2,512]{2,1,0:T(2,128)(2,1)} %reshape.203), calls=%async_computation.1 | async-start | bytes 524288 | tf_op jit(solution)/shard_map/all_to_all | solution.py:108
  69.4 22.0 %all-to-all-start.3 = ((bf16[128,2,512]{2,1,0:T(2,128)(2,1)}), bf16[128,2,512]{2,1,0:T(2,128)(2,1)S(1)}, u32[]{:S(2)}, u32[]{:S(2)}) async-start(bf16[128,2,512]{2,1,0:T(2,128)(2,1)} %reshape.207), calls=%async_computation.3 | async-start | bytes 524288 | tf_op jit(solution)/shard_map/all_to_all | solution.py:111
  79.0 95.7 %copy-start.9 = (pred[512,512]{0,1:T(8,128)(4,1)}, pred[512,512]{0,1:T(8,128)(4,1)S(1)}, u32[]{:S(2)}) copy-start(pred[512,512]{0,1:T(8,128)(4,1)S(1)} %copy.71) | copy-start | bytes 786436
  84.7 10.0 %copy-start.3 = (bf16[128,4,2,128]{0,3,2,1:T(8,128)(2,1)}, bf16[128,4,2,128]{0,3,2,1:T(8,128)(2,1)S(1)}, u32[]{:S(2)}) copy-start(bf16[128,4,2,128]{0,3,2,1:T(8,128)(2,1)S(1)} %copy.90) | copy-start | bytes 786436
  93.8 11.2 %copy-start.10 = (bf16[1,1,512,256]{2,3,1,0:T(8,128)(2,1)S(1)}, bf16[1,1,512,256]{2,3,1,0:T(8,128)(2,1)}, u32[]{:S(2)}) copy-start(bf16[1,1,512,256]{2,3,1,0:T(8,128)(2,1)} %copy.121) | copy-start | bytes 786436
  95.9 68.1 %all-to-all-start.7 = ((bf16[1,128,4,256]{3,2,0,1:T(4,128)(2,1)}), bf16[1,128,4,256]{3,2,0,1:T(4,128)(2,1)S(1)}, u32[]{:S(2)}, u32[]{:S(2)}) async-start(bf16[1,128,4,256]{3,2,0,1:T(4,128)(2,1)} %copy.106), calls=%async_computation.7 | async-start | bytes 524288 | tf_op jit(solution)/shard_map/all_to_all | solution.py:129
  159.7 15.0 %copy-start.11 = (bf16[1,1,512,256]{2,3,1,0:T(8,128)(2,1)S(1)}, bf16[1,1,512,256]{2,3,1,0:T(8,128)(2,1)}, u32[]{:S(2)}) copy-start(bf16[1,1,512,256]{2,3,1,0:T(8,128)(2,1)} %copy.121) | copy-start | bytes 786436
  163.9 24.2 %all-to-all-start.2 = ((bf16[128,2,512]{2,1,0:T(2,128)(2,1)}), bf16[128,2,512]{2,1,0:T(2,128)(2,1)S(1)}, u32[]{:S(2)}, u32[]{:S(2)}) async-start(bf16[128,2,512]{2,1,0:T(2,128)(2,1)} %reshape.205), calls=%async_computation.2 | async-start | bytes 524288 | tf_op jit(solution)/shard_map/all_to_all | solution.py:121
  174.6 299.3 %all-reduce.2.cloned.1.call-start = ((), (), s32[]{:S(2)}) async-start(), calls=%async_computation.8 | async-start | bytes 4194304 | tf_op jit(solution)/shard_map/psum | solution.py:153
  190.4 10.1 %copy-start.8 = (f32[4,2,128,128]{2,3,1,0:T(8,128)}, f32[4,2,128,128]{2,3,1,0:T(8,128)S(1)}, u32[]{:S(2)}) copy-start(f32[4,2,128,128]{2,3,1,0:T(8,128)S(1)} %fusion.84) | copy-start | bytes 1572868
  193.1 20.9 %all-to-all-start.5 = ((bf16[1,128,4,256]{3,2,0,1:T(4,128)(2,1)}), bf16[1,128,4,256]{3,2,0,1:T(4,128)(2,1)}, u32[]{:S(2)}, u32[]{:S(2)}) async-start(bf16[1,128,4,256]{3,2,0,1:T(4,128)(2,1)} %copy.96), calls=%async_computation.5 | async-start | bytes 524288 | tf_op jit(solution)/shard_map/all_to_all | solution.py:131
  202.0 20.6 %copy-start.13 = (bf16[1,1,512,256]{2,3,1,0:T(8,128)(2,1)S(1)}, bf16[1,1,512,256]{2,3,1,0:T(8,128)(2,1)}, u32[]{:S(2)}) copy-start(bf16[1,1,512,256]{2,3,1,0:T(8,128)(2,1)} %copy.120) | copy-start | bytes 786436
  213.9 22.1 %all-to-all-start.4 = ((bf16[1,128,4,256]{3,2,0,1:T(4,128)(2,1)}), bf16[1,128,4,256]{3,2,0,1:T(4,128)(2,1)}, u32[]{:S(2)}, u32[]{:S(2)}) async-start(bf16[1,128,4,256]{3,2,0,1:T(4,128)(2,1)} %copy.91), calls=%async_computation.4 | async-start | bytes 524288 | tf_op jit(solution)/shard_map/all_to_all | solution.py:130
  228.4 5.0 %copy-start.5 = (bf16[128,4,2,128]{0,3,2,1:T(8,128)(2,1)S(1)}, bf16[128,4,2,128]{0,3,2,1:T(8,128)(2,1)}, u32[]{:S(2)}) copy-start(bf16[128,4,2,128]{0,3,2,1:T(8,128)(2,1)} %copy-done.4) | copy-start | bytes 786436
  232.2 19.1 %copy-start.2 = (bf16[1,1,512,256]{2,3,1,0:T(8,128)(2,1)S(1)}, bf16[1,1,512,256]{2,3,1,0:T(8,128)(2,1)}, u32[]{:S(2)}) copy-start(bf16[1,1,512,256]{2,3,1,0:T(8,128)(2,1)} %get-tuple-element.8) | copy-start | bytes 786436
  232.3 19.1 %copy-start.12 = (bf16[1,1,512,256]{2,3,1,0:T(8,128)(2,1)S(1)}, bf16[1,1,512,256]{2,3,1,0:T(8,128)(2,1)}, u32[]{:S(2)}) copy-start(bf16[1,1,512,256]{2,3,1,0:T(8,128)(2,1)} %copy.121) | copy-start | bytes 786436
  236.0 242.9 %all-to-all-start.6 = ((bf16[1,128,4,256]{3,2,0,1:T(4,128)(2,1)}), bf16[1,128,4,256]{3,2,0,1:T(4,128)(2,1)S(1)}, u32[]{:S(2)}, u32[]{:S(2)}) async-start(bf16[1,128,4,256]{3,2,0,1:T(4,128)(2,1)} %copy.101), calls=%async_computation.6 | async-start | bytes 524288 | tf_op jit(solution)/shard_map/all_to_all | solution.py:132
  251.4 225.9 %copy-start.6 = (bf16[1,1,512,256]{3,2,1,0:T(8,128)(2,1)S(1)}, bf16[1,1,512,256]{3,2,1,0:T(8,128)(2,1)}, u32[]{:S(2)}) copy-start(bf16[1,1,512,256]{3,2,1,0:T(8,128)(2,1)} %copy.92) | copy-start | bytes 786436
  (2 other events, 5.0 us)
Sparse Core Ops, SparseCore 0:
  39.1 118.4 all-gather.2
Sparse Core Ops, SparseCore 1:
  180.0 293.8 all-reduce.1
where the time goes:
time: 497 us; the launch traced here: 488 us
  waiting for transfers between devices  311 us (63%)
  starting transfers between devices  88.5 us (18%)
  local copies, waits for them, and re-layouts  31.6 us (6%)
  matrix products  27.8 us (6%)
  between operations  16.3 us (3%)
  other arithmetic  12.3 us (2%)
    psum x1, waiting for transfers between devices, body(): summed = lax.psum(full_term, ('seq', 'rep'))  220 us
    all_gather x1, waiting for transfers between devices, body(): lax.all_gather(out_weight, 'seq', axis=0, tiled=True)  49.2 us
    all_to_all x1, starting transfers between devices, body(): lax.all_to_all(queries[..., row_width:], 'seq', split_axis=2, concat_axis...  20.9 us
    all_to_all x1, starting transfers between devices, body(): lax.all_to_all(column_results[3], 'seq', split_axis=1, concat_axis=2, til...  15.3 us
    all_to_all x1, starting transfers between devices, body(): lax.all_to_all(attn_grad[..., row_width:], 'seq', split_axis=2, concat_ax...  10.7 us
  transfers between devices with their start and end apart: 10, of which 8 were waited for; matrix products, arithmetic and copies ran while one was open for 13% of the time, Pallas kernels for 0%

commit v1 on v0

v1 whole, which is shorter than its diff:
```python
import functools
import math

import jax
import jax.numpy as jnp
from jax import lax
from jax.experimental import pallas as pl
from jax.experimental.pallas import tpu as pltpu
from jax.sharding import PartitionSpec as P

MESH = pl.DeviceIdType.MESH
F32 = jnp.float32
BF16 = jnp.bfloat16
NEG = -1e30

HEAD = 128
SCALE = 1.0 / math.sqrt(HEAD)
COLS = 512
FEAT = 512
MODEL = 1024
SEQ = 128
STEP = 37

W_Z, W_Y, W_X, W_C, G_1, G_2, B_1, B_2, S_C, S_X, S_Y, S_Z, S_R = range(13)


def nn(a, b):
    return lax.dot_general(a, b, (((1,), (0,)), ((), ())), preferred_element_type=F32)


def nt(a, b):
    return lax.dot_general(a, b, (((1,), (1,)), ((), ())), preferred_element_type=F32)


def tn(a, b):
    return lax.dot_general(a, b, (((0,), (0,)), ((), ())), preferred_element_type=F32)


def kernel(
    factor,
    q_hbm, k_hbm, v_hbm, g_hbm, w_hbm, row_tab, col_tab,
    dq_ref, dk_ref, dv_ref, wg_ref,
    q_ref, k_ref, v_ref, g_ref, w_ref,
    w_f32, w_piece, w_z, w_zf, w_qf, w_q, w_x,
    perm, row_bias, col_bias,
    grad, out, probs, dk_acc, dv_acc,
    send1, send2, recv1, recv2, back1, back2, got1, got2,
    stage, stage2, unit_q, unit_k, unit_v, unit_g, unit_p,
    op_t, wg_f, wg_s, wg_c, wg_b, wg_x, wg_cs, wg_y, wg_d, wg_z, wg_e, wg_r,
    in_sem, send_sem, recv_sem,
):
    seq = lax.axis_index("seq")
    rep = lax.axis_index("rep")
    z, y, xh = seq // 16, (seq // 2) % 8, seq % 2
    xl, core = rep // 2, rep % 2

    def place(zz, yy, xx):
        return zz * 16 + yy * 2 + xx

    def turned(step):
        return place((z + step // 16) % 8, (y + (step // 2) % 8) % 8, (xh + step) % 2)

    def remote(src, dst, which, to_seq, to_rep):
        return pltpu.make_async_remote_copy(
            src_ref=src, dst_ref=dst, send_sem=send_sem.at[which], recv_sem=recv_sem.at[which],
            device_id={"seq": to_seq, "rep": to_rep}, device_id_type=MESH,
        )

    def arrived(ref, which):
        pltpu.make_async_copy(ref, ref, recv_sem.at[which]).wait()

    def sent(ref, which):
        pltpu.make_async_copy(ref, ref, send_sem.at[which]).wait()

    loads = [
        pltpu.make_async_copy(a, b, in_sem.at[i])
        for i, (a, b) in enumerate(
            ((w_hbm, w_ref), (q_hbm, q_ref), (k_hbm, k_ref), (v_hbm, v_ref), (g_hbm, g_ref))
        )
    ]
    for load in loads:
        load.start()

    barrier = pltpu.get_barrier_semaphore()

    def greet(to_seq, to_rep):
        pl.semaphore_signal(
            barrier, inc=1, device_id={"seq": to_seq, "rep": to_rep}, device_id_type=MESH
        )

    def greet_step(j, carry):
        greet(turned(j), rep)
        return carry

    lax.fori_loop(1, SEQ, greet_step, 0)
    rep_core = xl * 2 + (1 - core)
    rep_x = (1 - xl) * 2 + core
    rep_both = (1 - xl) * 2 + (1 - core)
    seq_x = place(z, y, 1 - xh)
    greet(seq, rep_core)
    greet(seq, rep_x)
    greet(seq, rep_both)
    greet(seq_x, rep_x)

    loads[0].wait()
    w_val = w_ref[...].astype(F32)
    for b in range(8):
        w_f32[4 * b : 4 * b + 4, :] = w_val[:, 128 * b : 128 * b + 128]
    w_piece[...] = w_f32[...].astype(BF16)
    w_z[pl.ds(z, 1)] = w_piece[...][None]

    def pack(send, first, second):
        for h in range(2):
            lanes = slice(256 + 128 * h, 384 + 128 * h)
            for c in range(4):
                rows = slice(128 * c, 128 * c + 128)
                a = first[rows, lanes].astype(F32).reshape(16, 8, 128)
                b = second[rows, lanes].astype(F32).reshape(16, 8, 128)
                send[64 * h + 16 * c : 64 * h + 16 * c + 16] = jnp.concatenate(
                    (a, b), axis=1
                ).astype(BF16)

    loads[1].wait()
    loads[2].wait()
    pack(send1, q_ref, k_ref)
    recv1[pl.ds(seq, 1)] = send1[pl.ds(seq, 1)]

    def exchange(send, recv, which, low, high):
        def step(j, carry):
            to = turned((j * STEP) % SEQ)
            remote(send.at[to], recv.at[seq], which, to, rep).start()
            return carry

        lax.fori_loop(low, high, step, 0)

    pl.semaphore_wait(barrier, SEQ - 1 + 4)

    for d in (1, 7, 2, 6, 3, 5, 4):
        remote(w_piece, w_z.at[z], W_Z, place((z + d) % 8, y, xh), rep).start()
    exchange(send1, recv1, G_1, 1, 33)

    lane = lax.broadcasted_iota(jnp.int32, (64, 128), 1)
    row = lax.broadcasted_iota(jnp.int32, (64, 128), 0)
    for i in range(8):
        for j in range(i // 2 + 1):
            left = (row_tab[i, 2 * j].astype(F32) - 1.0) * -NEG
            right = (row_tab[i, 2 * j + 1].astype(F32) - 1.0) * -NEG
            bias = jnp.where(lane < 64, left, right)
            if j == i // 2:
                bias = jnp.where(lane + 128 * j <= row + 64 * i, bias, NEG)
            row_bias[64 * i : 64 * i + 64, 128 * j : 128 * j + 128] = bias
    lane = lax.broadcasted_iota(jnp.int32, (16, 128), 1)
    row = lax.broadcasted_iota(jnp.int32, (16, 128), 0)
    for i in range(8):
        bias = jnp.full((16, 128), NEG, F32)
        for j in range(i + 1):
            seen = (col_tab[i, j].astype(F32) - 1.0) * -NEG
            bias = jnp.where(lane // 16 == j, seen, bias)
        col_bias[16 * i : 16 * i + 16, :] = jnp.where(lane <= row + 16 * i, bias, NEG)
    for c in range(8):
        p = lax.broadcasted_iota(jnp.int32, (64, FEAT), 0) + 64 * c
        d = lax.broadcasted_iota(jnp.int32, (64, FEAT), 1)
        natural = ((p >> 2) & 7) * 64 + ((p >> 5) & 7) * 8 + (p >> 8) * 4 + (p & 3)
        perm[64 * c : 64 * c + 64, :] = jnp.where(natural == d, 1.0, 0.0).astype(BF16)

    def row_forward(h):
        lanes = slice(128 * h, 128 * h + 128)
        for b in range(4):
            n = 128 * (b + 1)
            rows = slice(128 * b, n)
            s = nt(q_ref[rows, lanes], k_ref[:n, lanes]) * SCALE + row_bias[rows, :n]
            e = jnp.exp(s - jnp.max(s, axis=1, keepdims=True))
            p = e * (1.0 / jnp.sum(e, axis=1, keepdims=True))
            probs[h, rows, :n] = p
            out[rows, lanes] = nn(p.astype(BF16), v_ref[:n, lanes]).astype(BF16)

    def row_backward(h):
        lanes = slice(128 * h, 128 * h + 128)
        for b in (3, 2, 1, 0):
            n = 128 * (b + 1)
            rows = slice(128 * b, n)
            p = probs[h, rows, :n]
            g = grad[rows, lanes]
            dp = nt(g, v_ref[:n, lanes])
            inner = jnp.sum(p * dp, axis=1, keepdims=True)
            ds = (p * (dp - inner) * SCALE).astype(BF16)
            dq_ref[rows, lanes] = nn(ds, k_ref[:n, lanes]).astype(BF16)
            dv = tn(p.astype(BF16), g)
            dk = tn(ds, q_ref[rows, lanes])
            if b == 3:
                dv_acc[...] = dv
                dk_acc[...] = dk
            else:
                dv_acc[:n, :] += dv
                dk_acc[:n, :] += dk
        dv_ref[:, lanes] = dv_acc[...].astype(BF16)
        dk_ref[:, lanes] = dk_acc[...].astype(BF16)

    arrived(w_z.at[pl.ds(0, 7)], W_Z)
    w_zf[...] = w_z[...].astype(F32).reshape(256, 128)
    for zz in range(8):
        part = w_zf[pl.ds(pl.multiple_of(32 * zz + 8 * rep, 8), 8), :]
        w_qf[4 * zz : 4 * zz + 4, 0:128] = part[0:4]
        w_qf[4 * zz : 4 * zz + 4, 128:256] = part[4:8]
    w_q[...] = w_qf[...].astype(BF16)

    def x_rows(which):
        return pl.ds(pl.multiple_of(which * 256, 256), 256)

    def y_rows(hi, lo):
        return pl.ds(pl.multiple_of(hi * 256 + lo * 32, 32), 32)

    w_x[rep, y_rows(xh, y), :] = w_q[...]
    for d in (1, 7, 2, 6, 3, 5, 4):
        remote(
            w_q, w_x.at[rep, y_rows(xh, y)], W_Y, place(z, (y + d) % 8, xh), rep
        ).start()
    exchange(send1, recv1, G_1, 33, 65)
    loads[3].wait()
    row_forward(0)
    arrived(w_x.at[0, pl.ds(0, 224)], W_Y)
    mine = w_x.at[rep, x_rows(xh)]
    remote(mine, mine, W_X, seq, rep_x).start()
    remote(mine, mine, W_X, seq_x, rep).start()
    remote(mine, mine, W_X, seq_x, rep_x).start()
    exchange(send1, recv1, G_1, 65, 97)
    row_forward(1)
    arrived(w_x.at[pl.ds(0, 3), pl.ds(0, 256)], W_X)
    remote(w_x.at[core], w_x.at[core], W_C, seq, rep_core).start()
    remote(w_x.at[2 + core], w_x.at[2 + core], W_C, seq, rep_core).start()
    exchange(send1, recv1, G_1, 97, SEQ)
    loads[4].wait()
    arrived(w_x.at[pl.ds(0, 2)], W_C)

    for c in range(4):
        rows = slice(128 * c, 128 * c + 128)
        total = nt(g_ref[rows, 0:256], w_x[0])
        for r in range(1, 4):
            total += nt(g_ref[rows, 256 * r : 256 * r + 256], w_x[r])
        grad[rows, :] = nn(total.astype(BF16), perm[...]).astype(BF16)
    pack(send2, v_ref, grad)
    recv2[pl.ds(seq, 1)] = send2[pl.ds(seq, 1)]
    exchange(send2, recv2, G_2, 1, SEQ)

    row_backward(0)
    row_backward(1)

    def spread(recv):
        for c in range(8):
            stage[256 * c : 256 * c + 256, :] = (
                recv[16 * c : 16 * c + 16].astype(F32).reshape(256, 128)
            )

    def gather(send):
        for c in range(8):
            send[16 * c : 16 * c + 16] = (
                stage2[256 * c : 256 * c + 256, :].reshape(16, 16, 128).astype(BF16)
            )

    def unit(u):
        return pl.ds(u, 128, stride=16)

    arrived(recv1.at[pl.ds(0, SEQ - 1)], G_1)
    spread(recv1)
    for u in range(8):
        q = stage[unit(u), :].astype(BF16)
        k = stage[unit(8 + u), :].astype(BF16)
        unit_q[u] = q
        unit_k[u] = k
        s = nt(q, k) * SCALE + col_bias[...]
        e = jnp.exp(s - jnp.max(s, axis=1, keepdims=True))
        unit_p[u] = e * (1.0 / jnp.sum(e, axis=1, keepdims=True))

    arrived(recv2.at[pl.ds(0, SEQ - 1)], G_2)
    spread(recv2)
    for u in range(8):
        v = stage[unit(u), :].astype(BF16)
        g = stage[unit(8 + u), :].astype(BF16)
        unit_v[u] = v
        unit_g[u] = g
        p = unit_p[u].astype(BF16)
        stage2[unit(u), :] = nn(p, v)
        stage2[unit(8 + u), :] = tn(p, g)
    gather(back1)
    got1[pl.ds(seq, 1)] = back1[pl.ds(seq, 1)]
    exchange(back1, got1, B_1, 1, SEQ)
    for u in range(8):
        p = unit_p[u]
        dp = nt(unit_g[u], unit_v[u])
        inner = jnp.sum(p * dp, axis=1, keepdims=True)
        ds = (p * (dp - inner) * SCALE).astype(BF16)
        stage2[unit(u), :] = nn(ds, unit_k[u])
        stage2[unit(8 + u), :] = tn(ds, unit_q[u])
    gather(back2)
    got2[pl.ds(seq, 1)] = back2[pl.ds(seq, 1)]
    exchange(back2, got2, B_2, 1, SEQ)

    def unpack(got, first, second):
        for h in range(2):
            lanes = slice(256 + 128 * h, 384 + 128 * h)
            for c in range(4):
                rows = slice(128 * c, 128 * c + 128)
                both = got[64 * h + 16 * c : 64 * h + 16 * c + 16].astype(F32)
                first[rows, lanes] = both[:, 0:8, :].reshape(128, 128).astype(BF16)
                second[rows, lanes] = both[:, 8:16, :].reshape(128, 128).astype(BF16)

    arrived(got1.at[pl.ds(0, SEQ - 1)], B_1)
    unpack(got1, out, dv_ref)

    for c in range(4):
        rows = slice(128 * c, 128 * c + 128)
        op_t[rows, :] = nt(perm[rows, :], out[...]).astype(BF16)
    for c in range(4):
        rows = slice(128 * c, 128 * c + 128)
        for r in range(4):
            term = nn(op_t[rows, :], g_ref[:, 256 * r : 256 * r + 256])
            wg_f[r, rows, :] = term
            wg_s[r, rows, :] = term.astype(BF16)
    remote(wg_s.at[1 - core], wg_c.at[0], S_C, seq, rep_core).start()
    remote(wg_s.at[3 - core], wg_c.at[1], S_C, seq, rep_core).start()
    arrived(wg_c, S_C)
    for i in range(2):
        for c in range(4):
            rows = slice(128 * c, 128 * c + 128)
            wg_b[i, rows, :] = (
                wg_f[2 * i + core, rows, :] + wg_c[i, rows, :].astype(F32)
            ).astype(BF16)
    here = xh * 2 + xl
    remote(wg_b.at[1 - xl, x_rows(xh)], wg_x.at[here], S_X, seq, rep_x).start()
    remote(wg_b.at[xl, x_rows(1 - xh)], wg_x.at[here], S_X, seq_x, rep).start()
    remote(wg_b.at[1 - xl, x_rows(1 - xh)], wg_x.at[here], S_X, seq_x, rep_x).start()
    wg_x[pl.ds(here, 1)] = wg_b[pl.ds(xl, 1), x_rows(xh), :]
    arrived(wg_x.at[pl.ds(0, 3)], S_X)
    total = wg_x[0].astype(F32)
    for i in range(1, 4):
        total += wg_x[i].astype(F32)
    wg_cs[...] = total.astype(BF16)
    for d in (1, 7, 2, 6, 3, 5, 4):
        to = (y + d) % 8
        remote(
            wg_cs.at[pl.ds(pl.multiple_of(to * 32, 32), 32)], wg_y.at[y], S_Y,
            place(z, to, xh), rep,
        ).start()
    wg_y[pl.ds(y, 1)] = wg_cs[pl.ds(pl.multiple_of(y * 32, 32), 32), :][None]
    arrived(wg_y.at[pl.ds(0, 7)], S_Y)
    total = wg_y[0].astype(F32)
    for i in range(1, 8):
        total += wg_y[i].astype(F32)
    wg_d[...] = total
    for d in (1, 7, 2, 6, 3, 5, 4):
        to = (z + d) % 8
        remote(
            wg_d.at[pl.ds(pl.multiple_of(to // 2 * 8, 8), 8)], wg_z.at[z], S_Z,
            place(to, y, xh), rep,
        ).start()
    wg_z[pl.ds(z, 1)] = wg_d[pl.ds(pl.multiple_of(z // 2 * 8, 8), 8), :][None]
    arrived(wg_z.at[pl.ds(0, 7)], S_Z)
    total = wg_z[0]
    for i in range(1, 8):
        total += wg_z[i]
    wg_e[...] = total * factor
    for to in (rep_core, rep_x, rep_both):
        remote(wg_e, wg_r.at[rep], S_R, seq, to).start()
    wg_r[pl.ds(rep, 1)] = wg_e[...][None]
    arrived(wg_r.at[pl.ds(0, 3)], S_R)
    odd = (z % 2) == 1
    for r in range(4):
        both = wg_r[r]
        wg_ref[:, 256 * r : 256 * r + 256] = jnp.where(odd, both[4:8, :], both[0:4, :])

    arrived(got2.at[pl.ds(0, SEQ - 1)], B_2)
    unpack(got2, dq_ref, dk_ref)

    sent(w_z.at[pl.ds(0, 7)], W_Z)
    sent(w_x.at[0, pl.ds(0, 224)], W_Y)
    sent(w_x.at[pl.ds(0, 3), pl.ds(0, 256)], W_X)
    sent(w_x.at[pl.ds(0, 2)], W_C)
    for which, ref in ((G_1, send1), (G_2, send2), (B_1, back1), (B_2, back2)):
        sent(ref.at[pl.ds(0, SEQ - 1)], which)
    sent(wg_c, S_C)
    sent(wg_x.at[pl.ds(0, 3)], S_X)
    sent(wg_y.at[pl.ds(0, 7)], S_Y)
    sent(wg_z.at[pl.ds(0, 7)], S_Z)
    sent(wg_r.at[pl.ds(0, 3)], S_R)


def body(queries, key_vectors, value_vectors, out_grad, out_weight, row_blocks, column_blocks):
    token_count = lax.axis_size("rep") * lax.axis_size("seq") * COLS
    factor = 1.0 / math.sqrt(token_count)
    vmem = pltpu.VMEM
    hbm = pl.BlockSpec(memory_space=pl.ANY)
    smem = pl.BlockSpec(memory_space=pltpu.SMEM)
    whole = pl.BlockSpec(memory_space=pltpu.VMEM)
    grads = jax.ShapeDtypeStruct((COLS, FEAT), BF16)
    pieces = vmem((SEQ, 16, 128), BF16)
    units = vmem((8, 128, 128), BF16)
    scratch = [
        vmem((COLS, FEAT), BF16), vmem((COLS, FEAT), BF16), vmem((COLS, FEAT), BF16),
        vmem((COLS, MODEL), BF16), vmem((4, MODEL), BF16),
        vmem((32, 128), F32), vmem((32, 128), BF16), vmem((8, 32, 128), BF16),
        vmem((256, 128), F32), vmem((32, 256), F32), vmem((32, 256), BF16),
        vmem((4, FEAT, 256), BF16),
        vmem((FEAT, FEAT), BF16), vmem((COLS, COLS), F32), vmem((SEQ, SEQ), F32),
        vmem((COLS, FEAT), BF16), vmem((COLS, FEAT), BF16), vmem((2, COLS, COLS), F32),
        vmem((COLS, HEAD), F32), vmem((COLS, HEAD), F32),
        pieces, pieces, pieces, pieces, pieces, pieces, pieces, pieces,
        vmem((SEQ * 16, 128), F32), vmem((SEQ * 16, 128), F32),
        units, units, units, units, vmem((8, 128, 128), F32),
        vmem((FEAT, COLS), BF16), vmem((4, FEAT, 256), F32), vmem((4, FEAT, 256), BF16),
        vmem((2, FEAT, 256), BF16), vmem((2, FEAT, 256), BF16), vmem((4, 256, 256), BF16),
        vmem((256, 256), BF16), vmem((8, 32, 256), BF16), vmem((32, 256), F32),
        vmem((8, 8, 256), F32), vmem((8, 256), F32), vmem((4, 8, 256), F32),
        pltpu.SemaphoreType.DMA((5,)),
        pltpu.SemaphoreType.DMA((13,)),
        pltpu.SemaphoreType.DMA((13,)),
    ]
    query_grad, key_grad, value_grad, weight_grad = pl.pallas_call(
        functools.partial(kernel, factor),
        out_shape=(grads, grads, grads, jax.ShapeDtypeStruct((4, MODEL), F32)),
        in_specs=[hbm] * 5 + [smem] * 2,
        out_specs=(whole, whole, whole, whole),
        scratch_shapes=scratch,
        compiler_params=pltpu.CompilerParams(
            collective_id=0, has_side_effects=True, vmem_limit_bytes=56 * 2**20
        ),
        cost_estimate=pl.CostEstimate(
            flops=2_500_000_000, bytes_accessed=5_000_000, transcendentals=800_000
        ),
    )(
        queries.reshape(COLS, FEAT), key_vectors.reshape(COLS, FEAT),
        value_vectors.reshape(COLS, FEAT), out_grad.reshape(COLS, MODEL),
        out_weight, row_blocks, column_blocks,
    )
    shape = (1, 1, COLS, FEAT)
    return (
        query_grad.reshape(shape), key_grad.reshape(shape), value_grad.reshape(shape), weight_grad
    )


def solution(mesh):
    return jax.shard_map(
        body,
        mesh=mesh,
        in_specs=(
            P("rep", "seq", None, None),
            P("rep", "seq", None, None),
            P("rep", "seq", None, None),
            P("rep", "seq", None, None),
            P("seq", None),
            P(),
            P(),
        ),
        out_specs=(
            P("rep", "seq", None, None),
            P("rep", "seq", None, None),
            P("rep", "seq", None, None),
            P("seq", None),
        ),
        check_vma=False,
    )
```

time: 497 us -> 117 us (0.24); the launches traced: 488 us -> 117 us
  waiting for transfers between devices: 311 us -> 0 us
  Pallas kernels: 0 us -> 111 us
  starting transfers between devices: 88.5 us -> 0 us
  matrix products: 27.8 us -> 0 us
  local copies, waits for them, and re-layouts: 31.6 us -> 4.56 us
  between operations: 16.3 us -> 0.65 us
  other arithmetic: 12.3 us -> 0 us
    psum x1 -> x0, waiting for transfers between devices: 220 us -> none  [body(): summed = lax.psum(full_term, ('seq', 'rep'))]
    pallas_call x0 -> x1, Pallas kernels: none -> 111 us  [body(): pl.pallas_call(functools.partial(kernel, factor), out_shape=(grads, grads...]
    all_to_all x8 -> x0, starting transfers between devices: 88.4 us -> none  [the longest x1 20.9 us: body(): lax.all_to_all(queries[..., row_width:], 'seq', split_axis=2, concat_axis...]
    all_gather x1 -> x0, waiting for transfers between devices: 49.2 us -> none  [body(): lax.all_gather(out_weight, 'seq', axis=0, tiled=True)]
    all_to_all x8 -> x0, waiting for transfers between devices: 41.3 us -> none  [the longest x1 9.75 us: body(): lax.all_to_all(queries[..., row_width:], 'seq', split_axis=2, concat_axis...]
    dot_general x15 -> x0, matrix products: 24.5 us -> none  [the longest x2 6.67 us: backward_pass(): jnp.einsum('nhqk,' + key_layout + '->' + layout, score_grad, key_in, pref...]
    unnamed x4 -> x0, other arithmetic: 8.85 us -> none
    reshape x16 -> x0, local copies, waits for them, and re-layouts: 8.73 us -> none  [the longest x4 4.47 us: column_back(): return tensor.reshape(1, all_rows, tensor.shape[1], strided_width)]
  transfers between devices with their start and end apart: 10 -> 0, of which waited for: 8 -> 0; matrix products, arithmetic and copies ran while one was open for 13% -> 0% of each run, Pallas kernels for 0% -> 0%
where the time goes in v1:
time: 117 us
  Pallas kernels  111 us (95%)
  local copies, waits for them, and re-layouts  4.56 us (4%)
    pallas_call x1, Pallas kernels, body(): pl.pallas_call(functools.partial(kernel, factor), out_shape=(grads, grads...  111 us
    unnamed x10, local copies, waits for them, and re-layouts  4.56 us

profile of v1, /device:TPU:1, one launch (start us, length us, event | category | flops | bytes accessed | tf_op | source)
XLA Modules:
  0.0 116.6 jit_solution(17836686080254054225)
XLA Ops:
  0.6 111.3 %shard_map.102 = (bf16[512,512]{1,0:T(8,128)(2,1)}, bf16[512,512]{1,0:T(8,128)(2,1)}, bf16[512,512]{1,0:T(8,128)(2,1)}, f32[4,1024]{1,0:T(4,128)}) custom-call(bf16[512,512]{1,0:T(8,128)(2,1)} %bitcast.11, bf16[512,512]{1,0:T(8,128)(2,1)} %bitcast.12, bf16[512,512]{1,0:T(8,128)(2,1)} %bitcast.13, bf16[512,1024]{1,0:T(8,128)(2,1)} %bitcast.10, ...), custom_call_target="tpu_custom_call" | custom-call | flops 2500000000 | bytes 5000000 | tf_op jit(solution)/shard_map/pallas_call | solution.py:417
  112.0 0.0 copy-start.1
  112.0 1.9 %copy.15 = bf16[1,1,512,512]{3,2,1,0:T(8,128)(2,1)} copy(bf16[1,1,512,512]{3,2,1,0:T(8,128)(2,1)} %bitcast.9) | data formatting | bytes 1048576
  113.9 0.0 copy-done.1
  113.9 0.0 copy-start
  113.9 0.8 copy.16
  114.7 0.4 copy-done
  115.2 0.0 copy-start.2
  115.2 0.8 copy.17
  116.0 0.0 copy-done.2
  116.0 0.6 copy.18
Async XLA Ops:
  112.0 1.9 %copy-start.1 = (bf16[512,512]{1,0:T(8,128)(2,1)S(1)}, bf16[512,512]{1,0:T(8,128)(2,1)}, u32[]{:S(2)}) copy-start(bf16[512,512]{1,0:T(8,128)(2,1)} %get-tuple-element.9) | copy-start | bytes 1572868
  113.9 1.2 %copy-start = (bf16[512,512]{1,0:T(8,128)(2,1)S(1)}, bf16[512,512]{1,0:T(8,128)(2,1)}, u32[]{:S(2)}) copy-start(bf16[512,512]{1,0:T(8,128)(2,1)} %get-tuple-element.10) | copy-start | bytes 1572868
  115.2 0.8 copy-start.2

commit v2 on v1

v2 whole, which is shorter than its diff:
```python
import functools
import math

import jax
import jax.numpy as jnp
from jax import lax
from jax.experimental import pallas as pl
from jax.experimental.pallas import tpu as pltpu
from jax.sharding import PartitionSpec as P

MESH = pl.DeviceIdType.MESH
F32 = jnp.float32
BF16 = jnp.bfloat16
NEG = -1e30

HEAD = 128
SCALE = 1.0 / math.sqrt(HEAD)
COLS = 512
FEAT = 512
MODEL = 1024
SEQ = 128

(
    W_ROW, W_STR, X_ROW, X_STR, C_ROW, C_STR, G_QK, G_V, G_G, B_O, B_V, B_QK,
    TC_ROW, TC_STR, TX_ROW, TX_STR, S_ALL, S_REP,
) = range(18)


def nn(a, b):
    return lax.dot_general(a, b, (((1,), (0,)), ((), ())), preferred_element_type=F32)


def nt(a, b):
    return lax.dot_general(a, b, (((1,), (1,)), ((), ())), preferred_element_type=F32)


def tn(a, b):
    return lax.dot_general(a, b, (((0,), (0,)), ((), ())), preferred_element_type=F32)


def kernel(
    factor,
    q_hbm, k_hbm, v_hbm, g_hbm, w_hbm, row_hbm, col_hbm,
    dq_ref, dk_ref, dv_ref, wg_ref,
    q_ref, k_ref, v_ref, g_ref, w_ref, row_tab, col_tab,
    w_f32, w_own, w_got, w_x, row_bias, col_bias,
    grad, out, probs, dk_acc, dv_acc,
    send_qk, send_v, send_g, recv_qk, recv_v, recv_g,
    back_o, back_v, back_qk, got_o, got_v, got_qk,
    stage, stage2, unit_q, unit_k, unit_v, unit_g, unit_p,
    term, term_b, term_got, term_own, term_away, term_near, sum_own, sum_got, last_own, last_got,
    in_sem, send_sem, recv_sem,
):
    seq = lax.axis_index("seq")
    rep = lax.axis_index("rep")
    z, y, xh = seq // 16, (seq // 2) % 8, seq % 2
    xl, core = rep // 2, rep % 2

    def remote(src, dst, which, to_seq, to_rep):
        return pltpu.make_async_remote_copy(
            src_ref=src, dst_ref=dst, send_sem=send_sem.at[which], recv_sem=recv_sem.at[which],
            device_id={"seq": to_seq, "rep": to_rep}, device_id_type=MESH,
        )

    def arrived(ref, which):
        pltpu.make_async_copy(ref, ref, recv_sem.at[which]).wait()

    def sent(ref, which):
        pltpu.make_async_copy(ref, ref, send_sem.at[which]).wait()

    loads = [
        pltpu.make_async_copy(a, b, in_sem.at[i])
        for i, (a, b) in enumerate(
            (
                (w_hbm, w_ref), (q_hbm, q_ref), (k_hbm, k_ref), (v_hbm, v_ref), (g_hbm, g_ref),
                (row_hbm, row_tab), (col_hbm, col_tab),
            )
        )
    ]
    for load in loads:
        load.start()

    around = [(d, x) for d in (4, 3, 5, 2, 6, 1, 7, 0) for x in (1, 0)]
    sides = [(((y + d) % 8) * 2 + (xh + x) % 2, 3 * (2 * d + x) + 1) for d, x in around]

    def rounds(one, low, high):
        def step(turn, carry):
            for i in range(16):
                one(((z + turn + sides[i][1]) % 8) * 16 + sides[i][0])
            return carry

        lax.fori_loop(low, min(high, 7), step, 0)
        if high == 8:
            for i in range(16):
                distance = (7 + sides[i][1]) % 8
                if around[i] != (0, 0) or distance != 0:
                    one(((z + distance) % 8) * 16 + sides[i][0])

    barrier = pltpu.get_barrier_semaphore()

    def greet(to_seq, to_rep):
        pl.semaphore_signal(
            barrier, inc=1, device_id={"seq": to_seq, "rep": to_rep}, device_id_type=MESH
        )

    rounds(lambda to: greet(to, rep), 0, 8)
    rep_core, rep_x = xl * 2 + (1 - core), (1 - xl) * 2 + core
    others = [rep_core, rep_x, (1 - xl) * 2 + (1 - core)]
    for to in others:
        greet(seq, to)

    loads[0].wait()
    w_val = w_ref[...].astype(F32)
    for b in range(8):
        w_f32[4 * b : 4 * b + 4, :] = w_val[:, 128 * b : 128 * b + 128]
    w_own[...] = w_f32[pl.ds(pl.multiple_of(8 * rep, 8), 8), :].astype(BF16)
    w_got[pl.ds(seq, 1)] = w_own[...][None]

    def pack(send, *tensors):
        for h in range(2):
            lanes = slice(256 + 128 * h, 384 + 128 * h)
            for c in range(4):
                rows = slice(128 * c, 128 * c + 128)
                parts = [t[rows, lanes].astype(F32).reshape(16, 8, 128) for t in tensors]
                whole = parts[0] if len(parts) == 1 else jnp.concatenate(parts, axis=1)
                send[64 * h + 16 * c : 64 * h + 16 * c + 16] = whole.astype(BF16)

    def keep(send, recv):
        recv[pl.ds(seq, 1)] = send[pl.ds(seq, 1)]

    loads[1].wait()
    loads[2].wait()
    pack(send_qk, q_ref, k_ref)
    keep(send_qk, recv_qk)
    loads[3].wait()
    pack(send_v, v_ref)
    keep(send_v, recv_v)

    def exchange(send, recv, which, low, high):
        def one(to):
            remote(send.at[to], recv.at[seq], which, to, rep).start()

        rounds(one, low, high)

    def share_weights(which):
        def one(to):
            remote(w_own, w_got.at[seq], which, to, rep).start()

        rounds(one, 0, 8)

    pl.semaphore_wait(barrier, SEQ - 1 + 3)

    def spread(recv, count):
        for c in range(8):
            stage[16 * count * c : 16 * count * (c + 1), :] = (
                recv[16 * c : 16 * c + 16].astype(F32).reshape(16 * count, 128)
            )

    def gather(send, count):
        for c in range(8):
            send[16 * c : 16 * c + 16] = (
                stage2[16 * count * c : 16 * count * (c + 1), :]
                .reshape(16, count, 128)
                .astype(BF16)
            )

    def unit(u, count):
        return pl.ds(u, 128, stride=count)

    def whole(ref):
        return ref.at[pl.ds(0, SEQ - 1)]

    strided = z >= 4

    @pl.when(strided)
    def _():
        share_weights(W_STR)

    exchange(send_qk, recv_qk, G_QK, 0, 8)

    loads[5].wait()
    loads[6].wait()
    lane = lax.broadcasted_iota(jnp.int32, (64, 128), 1)
    row = lax.broadcasted_iota(jnp.int32, (64, 128), 0)
    for i in range(8):
        for j in range(i // 2 + 1):
            left = (row_tab[i, 2 * j].astype(F32) - 1.0) * -NEG
            right = (row_tab[i, 2 * j + 1].astype(F32) - 1.0) * -NEG
            bias = jnp.where(lane < 64, left, right)
            if j == i // 2:
                bias = jnp.where(lane + 128 * j <= row + 64 * i, bias, NEG)
            row_bias[64 * i : 64 * i + 64, 128 * j : 128 * j + 128] = bias
    lane = lax.broadcasted_iota(jnp.int32, (16, 128), 1)
    row = lax.broadcasted_iota(jnp.int32, (16, 128), 0)
    for i in range(8):
        bias = jnp.full((16, 128), NEG, F32)
        for j in range(i + 1):
            seen = (col_tab[i, j].astype(F32) - 1.0) * -NEG
            bias = jnp.where(lane // 16 == j, seen, bias)
        col_bias[16 * i : 16 * i + 16, :] = jnp.where(lane <= row + 16 * i, bias, NEG)
    def row_forward(h):
        lanes = slice(128 * h, 128 * h + 128)
        for b in range(4):
            n = 128 * (b + 1)
            rows = slice(128 * b, n)
            s = nt(q_ref[rows, lanes], k_ref[:n, lanes]) * SCALE + row_bias[rows, :n]
            e = jnp.exp(s - jnp.max(s, axis=1, keepdims=True))
            p = e * (1.0 / jnp.sum(e, axis=1, keepdims=True))
            probs[h, rows, :n] = p
            out[rows, lanes] = nn(p.astype(BF16), v_ref[:n, lanes]).astype(BF16)

    def row_backward(h):
        lanes = slice(128 * h, 128 * h + 128)
        for b in (3, 2, 1, 0):
            n = 128 * (b + 1)
            rows = slice(128 * b, n)
            p = probs[h, rows, :n]
            g = grad[rows, lanes]
            dp = nt(g, v_ref[:n, lanes])
            inner = jnp.sum(p * dp, axis=1, keepdims=True)
            ds = (p * (dp - inner) * SCALE).astype(BF16)
            dq_ref[rows, lanes] = nn(ds, k_ref[:n, lanes]).astype(BF16)
            dv = tn(p.astype(BF16), g)
            dk = tn(ds, q_ref[rows, lanes])
            if b == 3:
                dv_acc[...] = dv
                dk_acc[...] = dk
            else:
                dv_acc[:n, :] += dv
                dk_acc[:n, :] += dk
        dv_ref[:, lanes] = dv_acc[...].astype(BF16)
        dk_ref[:, lanes] = dk_acc[...].astype(BF16)

    upper = lax.broadcasted_iota(jnp.int32, (32, 8, 128), 1) < 4

    def arrived_weights(which, mine, half):
        @pl.when(mine)
        def _():
            arrived(w_got.at[pl.ds(0, 63)], which)

        @pl.when(jnp.logical_not(mine))
        def _():
            arrived(w_got.at[pl.ds(0, 64)], which)

        pairs = w_got[64 * half : 64 * half + 64].astype(F32).reshape(32, 2, 8, 128)
        even, odd = pairs[:, 0], pairs[:, 1]
        left = jnp.where(upper, even, pltpu.roll(odd, 4, 1)).reshape(256, 128)
        right = jnp.where(upper, pltpu.roll(even, 4, 1), odd).reshape(256, 128)
        w_x[pl.ds(half, 1), pl.ds(rep, 1)] = (
            jnp.concatenate((left, right), axis=1).astype(BF16)[None, None]
        )

    def share_quarter(which_x, which_core, half):
        mine = w_x.at[half, rep]
        remote(mine, mine, which_x, seq, rep_x).start()
        remote(mine, mine, which_core, seq, rep_core).start()

    def relay_quarter(which_x, which_core, half):
        arrived(w_x.at[half, 0], which_x)
        theirs = w_x.at[half, rep_x]
        remote(theirs, theirs, which_core, seq, rep_core).start()

    def arrived_quarters(which_core, half):
        arrived(w_x.at[half, pl.ds(0, 2)], which_core)

    def quarters(ref):
        return ref.at[pl.ds(0, 3)]

    def attention_gradient(half):
        for c in range(4):
            rows = slice(128 * c, 128 * c + 128)
            total = nt(g_ref[rows, 0:256], w_x[half, 0])
            for r in range(1, 4):
                total += nt(g_ref[rows, 256 * r : 256 * r + 256], w_x[half, r])
            grad[rows, 256 * half : 256 * half + 256] = total.astype(BF16)

    def weight_terms(half, which):
        lanes = slice(256 * half, 256 * half + 256)
        for r in range(4):
            product = tn(out[:, lanes], g_ref[:, 256 * r : 256 * r + 256])
            term[half, r] = product
            term_b[half, r] = product.astype(BF16)
        for i in range(2):
            remote(
                term_b.at[half, 2 * i + 1 - core], term_got.at[half, i], which, seq, rep_core
            ).start()

    def chip_sums(half, which_core, which_x):
        arrived(term_got.at[half], which_core)
        term_own[half] = term[half, rep] + term_got[half, xl].astype(F32)
        term_away[half] = (term[half, rep_x] + term_got[half, 1 - xl].astype(F32)).astype(BF16)
        remote(term_away.at[half], term_near.at[half], which_x, seq, rep_x).start()

    def weight_sums(half, which_x):
        arrived(term_near.at[half], which_x)
        total = term_own[half] + term_near[half].astype(F32)
        left = total[:, 0:128].reshape(32, 8, 128)
        right = total[:, 128:256].reshape(32, 8, 128)
        even = jnp.where(upper, left, pltpu.roll(right, 4, 1))
        odd = jnp.where(upper, pltpu.roll(left, 4, 1), right)
        sum_own[64 * half : 64 * half + 64] = (
            jnp.stack((even, odd), axis=1).reshape(64, 8, 128).astype(BF16)
        )

        def one(to):
            remote(sum_own.at[to], sum_got.at[seq], S_ALL, to, rep).start()

        def step(turn, carry):
            for i in range(16):
                if around[i] != (0, 0):
                    one((4 * half + (z + turn + sides[i][1]) % 4) * 16 + sides[i][0])
            return carry

        lax.fori_loop(0, 4, step, 0)
        here = sides[-1][0]
        for d in (1, 2, 3):
            one((4 * half + (z + d) % 4) * 16 + here)
        mine = z // 4 == half

        @pl.when(jnp.logical_not(mine))
        def _():
            one((4 * half + z % 4) * 16 + here)

        @pl.when(mine)
        def _():
            sum_got[pl.ds(seq, 1)] = sum_own[pl.ds(seq, 1)]

    row_forward(0)
    row_forward(1)
    arrived_weights(W_STR, strided, 1)
    share_quarter(X_STR, C_STR, 1)
    exchange(send_v, recv_v, G_V, 0, 8)

    @pl.when(jnp.logical_not(strided))
    def _():
        share_weights(W_ROW)

    loads[4].wait()
    weight_terms(0, TC_ROW)
    relay_quarter(X_STR, C_STR, 1)
    chip_sums(0, TC_ROW, TX_ROW)
    arrived_quarters(C_STR, 1)
    attention_gradient(1)
    pack(send_g, grad)
    keep(send_g, recv_g)
    exchange(send_g, recv_g, G_G, 0, 8)

    arrived(whole(recv_qk), G_QK)
    spread(recv_qk, 16)
    for u in range(8):
        q = stage[unit(u, 16), :].astype(BF16)
        k = stage[unit(8 + u, 16), :].astype(BF16)
        unit_q[u] = q
        unit_k[u] = k
        s = nt(q, k) * SCALE + col_bias[...]
        e = jnp.exp(s - jnp.max(s, axis=1, keepdims=True))
        unit_p[u] = e * (1.0 / jnp.sum(e, axis=1, keepdims=True))
    arrived(whole(recv_v), G_V)
    spread(recv_v, 8)
    for u in range(8):
        v = stage[unit(u, 8), :].astype(BF16)
        unit_v[u] = v
        stage2[unit(u, 8), :] = nn(unit_p[u].astype(BF16), v)
    gather(back_o, 8)
    keep(back_o, got_o)
    sent(whole(send_qk), G_QK)
    sent(whole(send_v), G_V)
    exchange(back_o, got_o, B_O, 0, 8)

    arrived_weights(W_ROW, jnp.logical_not(strided), 0)
    share_quarter(X_ROW, C_ROW, 0)
    arrived(whole(recv_g), G_G)
    spread(recv_g, 8)
    for u in range(8):
        g = stage[unit(u, 8), :].astype(BF16)
        unit_g[u] = g
        stage2[unit(u, 8), :] = tn(unit_p[u].astype(BF16), g)
    gather(back_v, 8)
    keep(back_v, got_v)
    sent(whole(send_g), G_G)
    sent(whole(back_o), B_O)
    exchange(back_v, got_v, B_V, 0, 8)
    for u in range(8):
        p = unit_p[u]
        dp = nt(unit_g[u], unit_v[u])
        inner = jnp.sum(p * dp, axis=1, keepdims=True)
        ds = (p * (dp - inner) * SCALE).astype(BF16)
        stage2[unit(u, 16), :] = nn(ds, unit_k[u])
        stage2[unit(8 + u, 16), :] = tn(ds, unit_q[u])
    gather(back_qk, 16)
    keep(back_qk, got_qk)
    exchange(back_qk, got_qk, B_QK, 0, 8)

    def unpack(got, *tensors):
        for h in range(2):
            lanes = slice(256 + 128 * h, 384 + 128 * h)
            for c in range(4):
                rows = slice(128 * c, 128 * c + 128)
                part = got[64 * h + 16 * c : 64 * h + 16 * c + 16].astype(F32)
                for i, t in enumerate(tensors):
                    t[rows, lanes] = part[:, 8 * i : 8 * i + 8, :].reshape(128, 128).astype(BF16)

    relay_quarter(X_ROW, C_ROW, 0)
    weight_sums(0, TX_ROW)
    arrived(whole(got_o), B_O)
    unpack(got_o, out)
    weight_terms(1, TC_STR)
    arrived_quarters(C_ROW, 0)
    attention_gradient(0)
    chip_sums(1, TC_STR, TX_STR)
    row_backward(0)
    row_backward(1)
    weight_sums(1, TX_STR)

    arrived(whole(sum_got), S_ALL)
    total = sum_got[0:16].astype(F32)
    for i in range(1, 8):
        total += sum_got[16 * i : 16 * i + 16].astype(F32)
    total = jnp.sum(total, axis=0)
    last_own[...] = total * factor
    for to in others:
        remote(last_own, last_got.at[rep], S_REP, seq, to).start()
    last_got[pl.ds(rep, 1)] = last_own[...][None]
    arrived(quarters(last_got), S_REP)
    for r in range(4):
        wg_ref[:, 256 * r : 256 * r + 128] = last_got[r, 0:4, :]
        wg_ref[:, 256 * r + 128 : 256 * r + 256] = last_got[r, 4:8, :]

    arrived(whole(got_v), B_V)
    unpack(got_v, dv_ref)
    arrived(whole(got_qk), B_QK)
    unpack(got_qk, dq_ref, dk_ref)

    @pl.when(strided)
    def _():
        sent(whole(w_got), W_STR)

    @pl.when(jnp.logical_not(strided))
    def _():
        sent(whole(w_got), W_ROW)

    for half, which_x, which_core in ((0, X_ROW, C_ROW), (1, X_STR, C_STR)):
        sent(w_x.at[half, 0], which_x)
        sent(w_x.at[half, pl.ds(0, 2)], which_core)
    for which, ref in ((B_V, back_v), (B_QK, back_qk),):
        sent(whole(ref), which)
    for half, which_core, which_x in ((0, TC_ROW, TX_ROW), (1, TC_STR, TX_STR)):
        sent(term_got.at[half], which_core)
        sent(term_near.at[half], which_x)
    sent(whole(sum_got), S_ALL)
    sent(quarters(last_got), S_REP)


def finish(*refs):
    for i in range(4):
        refs[4 + i][...] = refs[i][...]


def body(queries, key_vectors, value_vectors, out_grad, out_weight, row_blocks, column_blocks):
    token_count = lax.axis_size("rep") * lax.axis_size("seq") * COLS
    factor = 1.0 / math.sqrt(token_count)
    vmem = pltpu.VMEM
    hbm = pl.BlockSpec(memory_space=pl.ANY)
    whole = pl.BlockSpec(memory_space=pltpu.VMEM)
    grads = jax.ShapeDtypeStruct((COLS, FEAT), BF16)
    one = vmem((SEQ, 8, 128), BF16)
    two = vmem((SEQ, 16, 128), BF16)
    units = vmem((8, 128, 128), BF16)
    scratch = [
        vmem((COLS, FEAT), BF16), vmem((COLS, FEAT), BF16), vmem((COLS, FEAT), BF16),
        vmem((COLS, MODEL), BF16), vmem((4, MODEL), BF16),
        pltpu.SMEM((8, 8), jnp.int32), pltpu.SMEM((8, 8), jnp.int32),
        vmem((32, 128), F32), vmem((8, 128), BF16), one, vmem((2, 4, 256, 256), BF16),
        vmem((COLS, COLS), F32), vmem((SEQ, SEQ), F32),
        vmem((COLS, FEAT), BF16), vmem((COLS, FEAT), BF16), vmem((2, COLS, COLS), F32),
        vmem((COLS, HEAD), F32), vmem((COLS, HEAD), F32),
        two, one, one, two, one, one, one, one, two, one, one, two,
        vmem((SEQ * 16, 128), F32), vmem((SEQ * 16, 128), F32),
        units, units, units, units, vmem((8, 128, 128), F32),
        vmem((2, 4, 256, 256), F32), vmem((2, 4, 256, 256), BF16), vmem((2, 2, 256, 256), BF16),
        vmem((2, 256, 256), F32), vmem((2, 256, 256), BF16), vmem((2, 256, 256), BF16),
        one, one, vmem((8, 128), F32), vmem((4, 8, 128), F32),
        pltpu.SemaphoreType.DMA((7,)),
        pltpu.SemaphoreType.DMA((18,)),
        pltpu.SemaphoreType.DMA((18,)),
    ]
    results = (grads, grads, grads, jax.ShapeDtypeStruct((4, MODEL), F32))
    raw = pl.pallas_call(
        functools.partial(kernel, factor),
        out_shape=results,
        in_specs=[hbm] * 7,
        out_specs=(whole, whole, whole, whole),
        scratch_shapes=scratch,
        compiler_params=pltpu.CompilerParams(
            collective_id=0, has_side_effects=True, vmem_limit_bytes=56 * 2**20
        ),
        cost_estimate=pl.CostEstimate(
            flops=2_500_000_000, bytes_accessed=5_000_000, transcendentals=800_000
        ),
    )(
        queries.reshape(COLS, FEAT), key_vectors.reshape(COLS, FEAT),
        value_vectors.reshape(COLS, FEAT), out_grad.reshape(COLS, MODEL),
        out_weight, row_blocks, column_blocks,
    )
    query_grad, key_grad, value_grad, weight_grad = pl.pallas_call(
        finish,
        out_shape=results,
        in_specs=[whole] * 4,
        out_specs=(whole,) * 4,
    )(*raw)
    shape = (1, 1, COLS, FEAT)
    return (
        query_grad.reshape(shape), key_grad.reshape(shape), value_grad.reshape(shape), weight_grad
    )


def solution(mesh):
    return jax.shard_map(
        body,
        mesh=mesh,
        in_specs=(
            P("rep", "seq", None, None),
            P("rep", "seq", None, None),
            P("rep", "seq", None, None),
            P("rep", "seq", None, None),
            P("seq", None),
            P(),
            P(),
        ),
        out_specs=(
            P("rep", "seq", None, None),
            P("rep", "seq", None, None),
            P("rep", "seq", None, None),
            P("seq", None),
        ),
        check_vma=False,
    )
```

time: 117 us -> 88.1 us (0.75)
  Pallas kernels: 111 us -> 87.4 us
  local copies, waits for them, and re-layouts: 4.56 us -> 0 us
    pallas_call x1 -> x2, Pallas kernels: 111 us -> 87.4 us  [the longest x1 84.8 us: body(): pl.pallas_call(functools.partial(kernel, factor), out_shape=results, in_s...]
    unnamed x10 -> x0, local copies, waits for them, and re-layouts: 4.56 us -> none
where the time goes in v2:
time: 88.1 us; the launch traced here: 88 us
  Pallas kernels  87.4 us (99%)
    pallas_call x1, Pallas kernels, body(): pl.pallas_call(functools.partial(kernel, factor), out_shape=results, in_s...  84.8 us
    pallas_call x1, Pallas kernels, body(): pl.pallas_call(finish, out_shape=results, in_specs=[whole] * 4, out_specs...  2.54 us

profile of v2, /device:TPU:1, one launch (start us, length us, event | category | flops | bytes accessed | tf_op | source)
XLA Modules:
  0.0 88.0 jit_solution(16576524898226536361)
XLA Ops:
  0.6 84.8 %shard_map.102 = (bf16[512,512]{1,0:T(8,128)(2,1)}, bf16[512,512]{1,0:T(8,128)(2,1)}, bf16[512,512]{1,0:T(8,128)(2,1)}, f32[4,1024]{1,0:T(4,128)}) custom-call(bf16[512,512]{1,0:T(8,128)(2,1)} %bitcast.8, bf16[512,512]{1,0:T(8,128)(2,1)} %bitcast.9, bf16[512,512]{1,0:T(8,128)(2,1)} %bitcast.10, bf16[512,1024]{1,0:T(8,128)(2,1)} %bitcast.7, ...), custom_call_target="tpu_custom_call" | custom-call | flops 2500000000 | bytes 5000000 | tf_op jit(solution)/shard_map/pallas_call | solution.py:488
  85.5 2.5 %shard_map.103 = (bf16[512,512]{1,0:T(8,128)(2,1)}, bf16[512,512]{1,0:T(8,128)(2,1)}, bf16[512,512]{1,0:T(8,128)(2,1)}, f32[4,1024]{1,0:T(4,128)}) custom-call(bf16[512,512]{1,0:T(8,128)(2,1)} %get-tuple-element.12.refs_0_, bf16[512,512]{1,0:T(8,128)(2,1)} %get-tuple-element.13.refs_1_, bf16[512,512]{1,0:T(8,128)(2,1)} %get-tuple-element.14.refs_2_, ...), custom_call_target="tpu_custom_call" | custom-call | tf_op jit(solution)/shard_map/pallas_call | solution.py:505

commit v3 on v2

--- a/solution.py
+++ b/solution.py
@@ -41,6 +41,7 @@
 def kernel(
     factor,
     q_hbm, k_hbm, v_hbm, g_hbm, w_hbm, row_hbm, col_hbm,
+    dq_hbm, dk_hbm, dv_hbm, wg_hbm,
     dq_ref, dk_ref, dv_ref, wg_ref,
     q_ref, k_ref, v_ref, g_ref, w_ref, row_tab, col_tab,
     w_f32, w_own, w_got, w_x, row_bias, col_bias,
@@ -49,7 +50,7 @@
     back_o, back_v, back_qk, got_o, got_v, got_qk,
     stage, stage2, unit_q, unit_k, unit_v, unit_g, unit_p,
     term, term_b, term_got, term_own, term_away, term_near, sum_own, sum_got, last_own, last_got,
-    in_sem, send_sem, recv_sem,
+    in_sem, out_sem, send_sem, recv_sem,
 ):
     seq = lax.axis_index("seq")
     rep = lax.axis_index("rep")
@@ -377,8 +378,6 @@
         stage2[unit(u, 8), :] = tn(unit_p[u].astype(BF16), g)
     gather(back_v, 8)
     keep(back_v, got_v)
-    sent(whole(send_g), G_G)
-    sent(whole(back_o), B_O)
     exchange(back_v, got_v, B_V, 0, 8)
     for u in range(8):
         p = unit_p[u]
@@ -411,6 +410,20 @@
     row_backward(0)
     row_backward(1)
     weight_sums(1, TX_STR)
+
+    stores = [
+        pltpu.make_async_copy(a, b, out_sem.at[i])
+        for i, (a, b) in enumerate(
+            ((dq_ref, dq_hbm), (dk_ref, dk_hbm), (dv_ref, dv_hbm), (wg_ref, wg_hbm))
+        )
+    ]
+    arrived(whole(got_v), B_V)
+    unpack(got_v, dv_ref)
+    stores[2].start()
+    arrived(whole(got_qk), B_QK)
+    unpack(got_qk, dq_ref, dk_ref)
+    stores[0].start()
+    stores[1].start()
 
     arrived(whole(sum_got), S_ALL)
     total = sum_got[0:16].astype(F32)
@@ -426,10 +439,9 @@
         wg_ref[:, 256 * r : 256 * r + 128] = last_got[r, 0:4, :]
         wg_ref[:, 256 * r + 128 : 256 * r + 256] = last_got[r, 4:8, :]
 
-    arrived(whole(got_v), B_V)
-    unpack(got_v, dv_ref)
-    arrived(whole(got_qk), B_QK)
-    unpack(got_qk, dq_ref, dk_ref)
+    stores[3].start()
+    for store in stores:
+        store.wait()
 
     @pl.when(strided)
     def _():
@@ -442,7 +454,7 @@
     for half, which_x, which_core in ((0, X_ROW, C_ROW), (1, X_STR, C_STR)):
         sent(w_x.at[half, 0], which_x)
         sent(w_x.at[half, pl.ds(0, 2)], which_core)
-    for which, ref in ((B_V, back_v), (B_QK, back_qk),):
+    for which, ref in ((G_G, send_g), (B_O, back_o), (B_V, back_v), (B_QK, back_qk)):
         sent(whole(ref), which)
     for half, which_core, which_x in ((0, TC_ROW, TX_ROW), (1, TC_STR, TX_STR)):
         sent(term_got.at[half], which_core)
@@ -452,8 +464,16 @@
 
 
 def finish(*refs):
-    for i in range(4):
-        refs[4 + i][...] = refs[i][...]
+    ins, outs, held, in_sem, out_sem = refs[:4], refs[4:8], refs[8:12], refs[12], refs[13]
+    into = [pltpu.make_async_copy(a, b, in_sem.at[i]) for i, (a, b) in enumerate(zip(ins, held))]
+    onto = [pltpu.make_async_copy(a, b, out_sem.at[i]) for i, (a, b) in enumerate(zip(held, outs))]
+    for copy in into:
+        copy.start()
+    for first, second in zip(into, onto):
+        first.wait()
+        second.start()
+    for copy in onto:
+        copy.wait()
 
 
 def body(queries, key_vectors, value_vectors, out_grad, out_weight, row_blocks, column_blocks):
@@ -461,12 +481,13 @@
     factor = 1.0 / math.sqrt(token_count)
     vmem = pltpu.VMEM
     hbm = pl.BlockSpec(memory_space=pl.ANY)
-    whole = pl.BlockSpec(memory_space=pltpu.VMEM)
     grads = jax.ShapeDtypeStruct((COLS, FEAT), BF16)
     one = vmem((SEQ, 8, 128), BF16)
     two = vmem((SEQ, 16, 128), BF16)
     units = vmem((8, 128, 128), BF16)
     scratch = [
+        vmem((COLS, FEAT), BF16), vmem((COLS, FEAT), BF16), vmem((COLS, FEAT), BF16),
+        vmem((4, MODEL), F32),
         vmem((COLS, FEAT), BF16), vmem((COLS, FEAT), BF16), vmem((COLS, FEAT), BF16),
         vmem((COLS, MODEL), BF16), vmem((4, MODEL), BF16),
         pltpu.SMEM((8, 8), jnp.int32), pltpu.SMEM((8, 8), jnp.int32),
@@ -481,6 +502,7 @@
         vmem((2, 256, 256), F32), vmem((2, 256, 256), BF16), vmem((2, 256, 256), BF16),
         one, one, vmem((8, 128), F32), vmem((4, 8, 128), F32),
         pltpu.SemaphoreType.DMA((7,)),
+        pltpu.SemaphoreType.DMA((4,)),
         pltpu.SemaphoreType.DMA((18,)),
         pltpu.SemaphoreType.DMA((18,)),
     ]
@@ -489,7 +511,7 @@
         functools.partial(kernel, factor),
         out_shape=results,
         in_specs=[hbm] * 7,
-        out_specs=(whole, whole, whole, whole),
+        out_specs=(hbm,) * 4,
         scratch_shapes=scratch,
         compiler_params=pltpu.CompilerParams(
             collective_id=0, has_side_effects=True, vmem_limit_bytes=56 * 2**20
@@ -505,8 +527,13 @@
     query_grad, key_grad, value_grad, weight_grad = pl.pallas_call(
         finish,
         out_shape=results,
-        in_specs=[whole] * 4,
-        out_specs=(whole,) * 4,
+        in_specs=[hbm] * 4,
+        out_specs=(hbm,) * 4,
+        scratch_shapes=[
+            vmem((COLS, FEAT), BF16), vmem((COLS, FEAT), BF16), vmem((COLS, FEAT), BF16),
+            vmem((4, MODEL), F32), pltpu.SemaphoreType.DMA((4,)), pltpu.SemaphoreType.DMA((4,)),
+        ],
+        compiler_params=pltpu.CompilerParams(vmem_limit_bytes=56 * 2**20),
     )(*raw)
     shape = (1, 1, COLS, FEAT)
     return (

time: 88.1 us -> 87.1 us (0.989)
  Pallas kernels: 87.4 us -> 86.3 us
where the time goes in v3:
time: 87.1 us; the launch traced here: 87 us
  Pallas kernels  86.3 us (99%)
    pallas_call x1, Pallas kernels, body(): pl.pallas_call(functools.partial(kernel, factor), out_shape=results, in_s...  84.1 us
    pallas_call x1, Pallas kernels, body(): pl.pallas_call(finish, out_shape=results, in_specs=[hbm] * 4, out_specs=(...  2.25 us

profile of v3, /device:TPU:1, one launch (start us, length us, event | category | flops | bytes accessed | tf_op | source)
XLA Modules:
  0.0 87.0 jit_solution(16715828451806242941)
XLA Ops:
  0.6 84.1 %shard_map.102 = (bf16[512,512]{1,0:T(8,128)(2,1)}, bf16[512,512]{1,0:T(8,128)(2,1)}, bf16[512,512]{1,0:T(8,128)(2,1)}, f32[4,1024]{1,0:T(4,128)}) custom-call(bf16[512,512]{1,0:T(8,128)(2,1)} %bitcast.8, bf16[512,512]{1,0:T(8,128)(2,1)} %bitcast.9, bf16[512,512]{1,0:T(8,128)(2,1)} %bitcast.10, bf16[512,1024]{1,0:T(8,128)(2,1)} %bitcast.7, ...), custom_call_target="tpu_custom_call" | custom-call | flops 2500000000 | bytes 5000000 | tf_op jit(solution)/shard_map/pallas_call | solution.py:510
  84.7 2.3 %shard_map.103 = (bf16[512,512]{1,0:T(8,128)(2,1)}, bf16[512,512]{1,0:T(8,128)(2,1)}, bf16[512,512]{1,0:T(8,128)(2,1)}, f32[4,1024]{1,0:T(4,128)}) custom-call(bf16[512,512]{1,0:T(8,128)(2,1)} %get-tuple-element.12.refs_0_, bf16[512,512]{1,0:T(8,128)(2,1)} %get-tuple-element.13.refs_1_, bf16[512,512]{1,0:T(8,128)(2,1)} %get-tuple-element.14.refs_2_, ...), custom_call_target="tpu_custom_call" | custom-call | tf_op jit(solution)/shard_map/pallas_call | solution.py:527

commit v4 on v3

--- a/solution.py
+++ b/solution.py
@@ -178,6 +178,7 @@
         share_weights(W_STR)
 
     exchange(send_qk, recv_qk, G_QK, 0, 8)
+    exchange(send_v, recv_v, G_V, 0, 4)
 
     loads[5].wait()
     loads[6].wait()
@@ -330,7 +331,7 @@
     row_forward(1)
     arrived_weights(W_STR, strided, 1)
     share_quarter(X_STR, C_STR, 1)
-    exchange(send_v, recv_v, G_V, 0, 8)
+    exchange(send_v, recv_v, G_V, 4, 8)
 
     @pl.when(jnp.logical_not(strided))
     def _():

time: 87.1 us -> 87.3 us (level)
  no operation moved by 1% of the time
where the time goes in v4:
time: 87.3 us; the launch traced here: 87.1 us
  Pallas kernels  86.5 us (99%)
    pallas_call x1, Pallas kernels, body(): pl.pallas_call(functools.partial(kernel, factor), out_shape=results, in_s...  84.3 us
    pallas_call x1, Pallas kernels, body(): pl.pallas_call(finish, out_shape=results, in_specs=[hbm] * 4, out_specs=(...  2.25 us

profile of v4, /device:TPU:1, one launch (start us, length us, event | category | flops | bytes accessed | tf_op | source)
XLA Modules:
  0.0 87.1 jit_solution(9891065712646700614)
XLA Ops:
  0.6 84.3 %shard_map.102 = (bf16[512,512]{1,0:T(8,128)(2,1)}, bf16[512,512]{1,0:T(8,128)(2,1)}, bf16[512,512]{1,0:T(8,128)(2,1)}, f32[4,1024]{1,0:T(4,128)}) custom-call(bf16[512,512]{1,0:T(8,128)(2,1)} %bitcast.8, bf16[512,512]{1,0:T(8,128)(2,1)} %bitcast.9, bf16[512,512]{1,0:T(8,128)(2,1)} %bitcast.10, bf16[512,1024]{1,0:T(8,128)(2,1)} %bitcast.7, ...), custom_call_target="tpu_custom_call" | custom-call | flops 2500000000 | bytes 5000000 | tf_op jit(solution)/shard_map/pallas_call | solution.py:511
  84.9 2.3 %shard_map.103 = (bf16[512,512]{1,0:T(8,128)(2,1)}, bf16[512,512]{1,0:T(8,128)(2,1)}, bf16[512,512]{1,0:T(8,128)(2,1)}, f32[4,1024]{1,0:T(4,128)}) custom-call(bf16[512,512]{1,0:T(8,128)(2,1)} %get-tuple-element.12.refs_0_, bf16[512,512]{1,0:T(8,128)(2,1)} %get-tuple-element.13.refs_1_, bf16[512,512]{1,0:T(8,128)(2,1)} %get-tuple-element.14.refs_2_, ...), custom_call_target="tpu_custom_call" | custom-call | tf_op jit(solution)/shard_map/pallas_call | solution.py:528
